TPU v7x, 512 devices: a whole 4x4x16 slice. The times are simulated.
512 devices in a mesh: row: 16 (over z), col: 16 (over y_hi, x, core), chan: 2 (over y_lo).
Axes of the slice: x: 4, y: 4 (y_hi: 2, y_lo: 2; y = y_hi * 2 + y_lo), z: 16, core: 2. Of those that a mesh axis runs over, the one named last changes fastest.
Arguments:
- array_volts: bfloat16 [6, 2, 2048, 2048], P('chan', None, ('row', 'col')), parts along dimension 0, may hold values from -15 to 15, as said below
- reference_volts: bfloat16 [6, 2, 32, 2048], P('chan', None, None, 'col'), parts along dimension 0, may hold values from -15 to 15, as said below
Outputs:
- cleaned: float32 [6, 2, 2048, 2048], P('chan', None, 'row', 'col'), parts along dimension 0
There are 2 independent parts, one for each index of `chan`. A program takes and returns all parts, laid end to end along the dimension named above; each array names one. Nothing has to cross between parts.
Inputs may be any that keep to these rules, and one draw needn't show every extreme that they name: `array_volts`: array voltages: common interference from a few sources plus independent noise. `reference_volts`: reference voltages: the same interference sources seen with other gains, plus independent noise.
All inputs are finite; a program needn't handle non-finite values.
Results may differ from a plain program's by a relative error of at most 0.0003.
Values may be sent and summed in bfloat16 or wider, within the bound.
A program may use at most 64 MiB of HBM per device.

v0:
```python
import jax
import jax.numpy as jnp
from jax import lax
from jax.sharding import PartitionSpec as P


def in_order(blocks, dim):
    shape = list(blocks.shape[1:])
    shape[dim] *= blocks.shape[0]
    return jnp.moveaxis(blocks, 0, dim).reshape(shape)


def sent_to_all(x, axis):
    copies = jnp.broadcast_to(x, (lax.axis_size(axis), *x.shape))
    return lax.all_to_all(copies, axis, split_axis=0, concat_axis=0, tiled=True)


def collect(x, axis, dim):
    return in_order(sent_to_all(x, axis), dim)


def correlate(first_rows, second_rows):
    width_first = first_rows.shape[1]
    width_second = second_rows.shape[1]
    samples = first_rows.shape[2]
    stacked_first = first_rows.reshape(2 * width_first, samples)
    stacked_second = second_rows.reshape(2 * width_second, samples)
    product = jnp.einsum(
        "xn,yn->xy", stacked_first, stacked_second, preferred_element_type=jnp.float32
    )
    real_part = product[:width_first, :width_second] + product[width_first:, width_second:]
    imaginary_portion = product[width_first:, :width_second] - product[:width_first, width_second:]
    return jnp.stack([real_part, imaginary_portion]) / jnp.float32(samples)


def subtract(vis_tile, rows_cross, cross_cols, reference_covariance):
    real_cov = reference_covariance[0]
    imag_cov = reference_covariance[1]
    system = jnp.concatenate(
        [jnp.concatenate([real_cov, -imag_cov], 1), jnp.concatenate([imag_cov, real_cov], 1)], 0
    )
    lower_factor = jnp.linalg.cholesky(system)
    right_hand = jnp.concatenate([cross_cols[0], cross_cols[1]], 0)
    middle = lax.linalg.triangular_solve(lower_factor, right_hand, left_side=True, lower=True)
    solved = lax.linalg.triangular_solve(
        lower_factor, middle, left_side=True, lower=True, transpose_a=True
    )
    half_size = real_cov.shape[0]
    solved_real = solved[:half_size]
    solved_imag = solved[half_size:]
    highest = lax.Precision.HIGHEST
    corr_real = jnp.dot(rows_cross[0], solved_real, precision=highest) - jnp.dot(
        rows_cross[1], solved_imag, precision=highest
    )
    corr_imag = jnp.dot(rows_cross[0], solved_imag, precision=highest) + jnp.dot(
        rows_cross[1], solved_real, precision=highest
    )
    return vis_tile - jnp.stack([corr_real, corr_imag])


def per_device(array_volts, reference_volts):
    results = []
    for sub_index in range(array_volts.shape[0]):
        local_volts = array_volts[sub_index]
        ref_all = collect(reference_volts[sub_index], "col", 2)
        reference_covariance = correlate(ref_all, ref_all)
        row_volts = collect(local_volts, "col", 1)
        width_rows = row_volts.shape[1]
        left_factor_matrix = jnp.concatenate([row_volts, ref_all], 1)
        joined = correlate(
            left_factor_matrix, lax.all_gather(local_volts, "row", axis=1, tiled=True)
        )
        vis_tile = joined[:, :width_rows]
        cross_cols = joined[:, width_rows:]
        rows_cross = correlate(row_volts, ref_all)
        results.append(subtract(vis_tile, rows_cross, cross_cols, reference_covariance))
    return jnp.stack(results)


def solution(mesh):
    return jax.shard_map(
        per_device,
        mesh=mesh,
        in_specs=(P("chan", None, ("row", "col"), None), P("chan", None, None, "col")),
        out_specs=P("chan", None, "row", "col"),
        check_vma=False,
    )
```

profile of v0, /device:TPU:2, one launch (start us, length us, event | category | flops | bytes accessed | tf_op | source)
XLA Modules:
  0.0 237.6 jit_solution(3841975494435622801)
XLA Ops:
  6.5 1.6 fusion.99
  8.2 0.7 all-gather.9.cloned.1.call-update
  8.9 0.8 slice_bitcast_fusion.20
  9.7 0.8 broadcast_in_dim.24
  10.4 9.2 %all-to-all-start.5 = ((bf16[16,2,32,128]{3,2,1,0:T(8,128)(2,1)}), bf16[16,2,32,128]{3,2,1,0:T(8,128)(2,1)S(1)}, u32[]{:S(2)}, u32[]{:S(2)}) async-start(bf16[16,2,32,128]{3,2,1,0:T(8,128)(2,1)} %broadcast_in_dim.24), calls=%async_computation.5 | async-start | bytes 524288 | tf_op jit(solution)/shard_map/all_to_all | solution.py:15
  19.7 0.7 all-gather.7.cloned.1.call-update
  20.4 6.3 %all-to-all-done.5 = bf16[16,2,32,128]{3,2,1,0:T(8,128)(2,1)S(1)} async-done(((bf16[16,2,32,128]{3,2,1,0:T(8,128)(2,1)}), bf16[16,2,32,128]{3,2,1,0:T(8,128)(2,1)S(1)}, u32[]{:S(2)}, u32[]{:S(2)}) %all-to-all-start.5) | async-done | bytes 262176 | tf_op jit(solution)/shard_map/all_to_all | solution.py:15
  26.7 0.8 broadcast_in_dim.22
  27.4 5.8 %all-to-all-start.3 = ((bf16[16,2,32,128]{3,2,1,0:T(8,128)(2,1)}), bf16[16,2,32,128]{3,2,1,0:T(8,128)(2,1)S(1)}, u32[]{:S(2)}, u32[]{:S(2)}) async-start(bf16[16,2,32,128]{3,2,1,0:T(8,128)(2,1)} %broadcast_in_dim.22), calls=%async_computation.3 | async-start | bytes 524288 | tf_op jit(solution)/shard_map/all_to_all | solution.py:15
  33.8 0.4 copy-done.2
  34.2 6.1 %all-to-all-done.3 = bf16[16,2,32,128]{3,2,1,0:T(8,128)(2,1)S(1)} async-done(((bf16[16,2,32,128]{3,2,1,0:T(8,128)(2,1)}), bf16[16,2,32,128]{3,2,1,0:T(8,128)(2,1)S(1)}, u32[]{:S(2)}, u32[]{:S(2)}) %all-to-all-start.3) | async-done | bytes 262176 | tf_op jit(solution)/shard_map/all_to_all | solution.py:15
  40.3 0.8 broadcast_in_dim.20
  41.1 5.8 %all-to-all-start.1 = ((bf16[16,2,32,128]{3,2,1,0:T(8,128)(2,1)}), bf16[16,2,32,128]{3,2,1,0:T(8,128)(2,1)S(1)}, u32[]{:S(2)}, u32[]{:S(2)}) async-start(bf16[16,2,32,128]{3,2,1,0:T(8,128)(2,1)} %broadcast_in_dim.20), calls=%async_computation.1 | async-start | bytes 524288 | tf_op jit(solution)/shard_map/all_to_all | solution.py:15
  47.4 0.4 copy-done.4
  47.8 6.2 %all-to-all-done.1 = bf16[16,2,32,128]{3,2,1,0:T(8,128)(2,1)S(1)} async-done(((bf16[16,2,32,128]{3,2,1,0:T(8,128)(2,1)}), bf16[16,2,32,128]{3,2,1,0:T(8,128)(2,1)S(1)}, u32[]{:S(2)}, u32[]{:S(2)}) %all-to-all-start.1) | async-done | bytes 262176 | tf_op jit(solution)/shard_map/all_to_all | solution.py:15
  54.0 1.1 broadcast_in_dim.23
  55.1 6.0 %all-to-all-start.4 = ((bf16[16,2,8,2048]{3,2,1,0:T(8,128)(2,1)}), bf16[16,2,8,2048]{3,2,1,0:T(8,128)(2,1)S(1)}, u32[]{:S(2)}, u32[]{:S(2)}) async-start(bf16[16,2,8,2048]{3,2,1,0:T(8,128)(2,1)} %broadcast_in_dim.23), calls=%async_computation.4 | async-start | bytes 2097152 | tf_op jit(solution)/shard_map/all_to_all | solution.py:15
  61.2 0.7 copy-done.6
  62.5 5.9 %cholesky.81 = f32[64,64]{1,0:T(8,128)S(1)} custom-call(f32[64,64]{1,0:T(8,128)S(1)} %fusion.51), custom_call_target="Cholesky" | custom-call | tf_op jit(solution)/shard_map/jit(cholesky)/cholesky | solution.py:42
  68.4 0.7 compare_reduce_fusion
  69.3 5.9 %cholesky.70 = f32[64,64]{1,0:T(8,128)S(1)} custom-call(f32[64,64]{1,0:T(8,128)S(1)} %fusion.55), custom_call_target="Cholesky" | custom-call | tf_op jit(solution)/shard_map/jit(cholesky)/cholesky | solution.py:42
  75.5 5.9 %cholesky.59 = f32[64,64]{1,0:T(8,128)S(1)} custom-call(f32[64,64]{1,0:T(8,128)S(1)} %fusion.59), custom_call_target="Cholesky" | custom-call | tf_op jit(solution)/shard_map/jit(cholesky)/cholesky | solution.py:42
  81.3 0.7 compare_reduce_fusion.1
  82.1 0.6 fusion.35
  82.7 0.6 fusion.34
  83.4 1.1 broadcast_in_dim.21
  84.5 7.3 %all-to-all-start.2 = ((bf16[16,2,8,2048]{3,2,1,0:T(8,128)(2,1)}), bf16[16,2,8,2048]{3,2,1,0:T(8,128)(2,1)S(1)}, u32[]{:S(2)}, u32[]{:S(2)}) async-start(bf16[16,2,8,2048]{3,2,1,0:T(8,128)(2,1)} %broadcast_in_dim.21), calls=%async_computation.2 | async-start | bytes 2097152 | tf_op jit(solution)/shard_map/all_to_all | solution.py:15
  91.8 0.7 compare_reduce_fusion.2
  92.4 0.7 copy_bitcast_fusion.1
  93.2 0.7 copy_bitcast_fusion.2
  93.9 12.8 %all-to-all-done.2 = bf16[16,2,8,2048]{3,2,1,0:T(8,128)(2,1)S(1)} async-done(((bf16[16,2,8,2048]{3,2,1,0:T(8,128)(2,1)}), bf16[16,2,8,2048]{3,2,1,0:T(8,128)(2,1)S(1)}, u32[]{:S(2)}, u32[]{:S(2)}) %all-to-all-start.2) | async-done | bytes 1048608 | tf_op jit(solution)/shard_map/all_to_all | solution.py:15
  106.7 1.1 broadcast_in_dim.19
  107.8 7.2 %all-to-all-start = ((bf16[16,2,8,2048]{3,2,1,0:T(8,128)(2,1)}), bf16[16,2,8,2048]{3,2,1,0:T(8,128)(2,1)}, u32[]{:S(2)}, u32[]{:S(2)}) async-start(bf16[16,2,8,2048]{3,2,1,0:T(8,128)(2,1)} %broadcast_in_dim.19), calls=%async_computation | async-start | bytes 2097152 | tf_op jit(solution)/shard_map/all_to_all | solution.py:15
  115.0 0.6 fusion.33
  115.7 4.9 %custom-call.17 = f32[1,64,64]{1,2,0:T(8,128)S(1)} custom-call(f32[1,64,64]{2,1,0:T(8,128)S(1)} %fusion.35), custom_call_target="InvertDiagBlocksLowerTriangular" | custom-call | tf_op jit(solution)/shard_map/triangular_solve/custom-call.2 | solution.py:45
  120.6 4.9 %custom-call.15 = f32[1,64,64]{1,2,0:T(8,128)S(1)} custom-call(f32[1,64,64]{2,1,0:T(8,128)S(1)} %fusion.34), custom_call_target="InvertDiagBlocksLowerTriangular" | custom-call | tf_op jit(solution)/shard_map/triangular_solve/custom-call.2 | solution.py:45
  125.5 4.9 %custom-call.13 = f32[1,64,64]{1,2,0:T(8,128)S(1)} custom-call(f32[1,64,64]{2,1,0:T(8,128)S(1)} %fusion.33), custom_call_target="InvertDiagBlocksLowerTriangular" | custom-call | tf_op jit(solution)/shard_map/triangular_solve/custom-call.2 | solution.py:45
  130.7 0.8 copy-done.3
  131.5 0.4 fusion.8
  132.0 0.4 fusion.12
  132.4 1.3 copy.120
  133.8 0.4 fusion.16
  134.3 1.2 pad_maximum_fusion.2
  135.6 0.8 copy-done
  136.5 2.2 fusion.102
  138.8 16.9 %all-gather.9.cloned.1.call-done = bf16[1,2,128,2048]{3,2,1,0:T(8,128)(2,1)} async-done(((bf16[1,2,8,2048]{3,2,1,0:T(8,128)(2,1)}), bf16[1,2,128,2048]{3,2,1,0:T(8,128)(2,1)}) %all-gather.9.cloned.1.call-update) | async-done | bytes 1048592 | tf_op jit(solution)/shard_map/all_gather | solution.py:71
  155.7 1.8 fusion.101
  157.5 0.2 fusion.44
  158.2 0.3 fusion.76
  158.5 0.3 fusion.77
  158.9 0.3 fusion.74
  159.2 0.3 fusion.75
  159.5 66.1 %all-gather.7.cloned.1.call-done = bf16[1,2,128,2048]{3,2,1,0:T(8,128)(2,1)} async-done(((bf16[1,2,8,2048]{3,2,1,0:T(8,128)(2,1)}), bf16[1,2,128,2048]{3,2,1,0:T(8,128)(2,1)}) %all-gather.7.cloned.1.call-update) | async-done | bytes 1048592 | tf_op jit(solution)/shard_map/all_gather | solution.py:71
  225.6 1.8 fusion.100
  227.4 0.2 fusion.36
  227.9 0.3 fusion.72
  228.2 0.3 fusion.73
  228.4 0.3 fusion
  228.7 0.3 fusion.1
  229.0 0.3 fusion.2
  229.3 0.3 fusion.3
  229.6 0.3 fusion.4
  229.9 0.3 fusion.5
  230.3 0.8 pad_maximum_fusion.3
  (74 shorter events, 3.8 us)
Async XLA Ops:
  6.5 130.0 %all-gather.11.cloned.1.call-start = ((), (), s32[]{:S(2)}) async-start(), calls=%async_computation.8 | async-start | bytes 1114112 | tf_op jit(solution)/shard_map/all_gather | solution.py:71
  8.2 147.5 %all-gather.9.cloned.1.call-start = ((), (), s32[]{:S(2)}) async-start(), calls=%async_computation.7 | async-start | bytes 1114112 | tf_op jit(solution)/shard_map/all_gather | solution.py:71
  10.4 16.3 %all-to-all-start.5 = ((bf16[16,2,32,128]{3,2,1,0:T(8,128)(2,1)}), bf16[16,2,32,128]{3,2,1,0:T(8,128)(2,1)S(1)}, u32[]{:S(2)}, u32[]{:S(2)}) async-start(bf16[16,2,32,128]{3,2,1,0:T(8,128)(2,1)} %broadcast_in_dim.24), calls=%async_computation.5 | async-start | bytes 524288 | tf_op jit(solution)/shard_map/all_to_all | solution.py:15
  19.7 206.0 %all-gather.7.cloned.1.call-start = ((), (), s32[]{:S(2)}) async-start(), calls=%async_computation.6 | async-start | bytes 1114112 | tf_op jit(solution)/shard_map/all_gather | solution.py:71
  27.4 12.9 %all-to-all-start.3 = ((bf16[16,2,32,128]{3,2,1,0:T(8,128)(2,1)}), bf16[16,2,32,128]{3,2,1,0:T(8,128)(2,1)S(1)}, u32[]{:S(2)}, u32[]{:S(2)}) async-start(bf16[16,2,32,128]{3,2,1,0:T(8,128)(2,1)} %broadcast_in_dim.22), calls=%async_computation.3 | async-start | bytes 524288 | tf_op jit(solution)/shard_map/all_to_all | solution.py:15
  33.5 0.7 copy-start.2
  41.1 12.9 %all-to-all-start.1 = ((bf16[16,2,32,128]{3,2,1,0:T(8,128)(2,1)}), bf16[16,2,32,128]{3,2,1,0:T(8,128)(2,1)S(1)}, u32[]{:S(2)}, u32[]{:S(2)}) async-start(bf16[16,2,32,128]{3,2,1,0:T(8,128)(2,1)} %broadcast_in_dim.20), calls=%async_computation.1 | async-start | bytes 524288 | tf_op jit(solution)/shard_map/all_to_all | solution.py:15
  47.1 0.7 copy-start.4
  55.1 28.3 %all-to-all-start.4 = ((bf16[16,2,8,2048]{3,2,1,0:T(8,128)(2,1)}), bf16[16,2,8,2048]{3,2,1,0:T(8,128)(2,1)S(1)}, u32[]{:S(2)}, u32[]{:S(2)}) async-start(bf16[16,2,8,2048]{3,2,1,0:T(8,128)(2,1)} %broadcast_in_dim.23), calls=%async_computation.4 | async-start | bytes 2097152 | tf_op jit(solution)/shard_map/all_to_all | solution.py:15
  61.2 0.7 copy-start.6
  84.5 22.2 %all-to-all-start.2 = ((bf16[16,2,8,2048]{3,2,1,0:T(8,128)(2,1)}), bf16[16,2,8,2048]{3,2,1,0:T(8,128)(2,1)S(1)}, u32[]{:S(2)}, u32[]{:S(2)}) async-start(bf16[16,2,8,2048]{3,2,1,0:T(8,128)(2,1)} %broadcast_in_dim.21), calls=%async_computation.2 | async-start | bytes 2097152 | tf_op jit(solution)/shard_map/all_to_all | solution.py:15
  107.8 24.6 %all-to-all-start = ((bf16[16,2,8,2048]{3,2,1,0:T(8,128)(2,1)}), bf16[16,2,8,2048]{3,2,1,0:T(8,128)(2,1)}, u32[]{:S(2)}, u32[]{:S(2)}) async-start(bf16[16,2,8,2048]{3,2,1,0:T(8,128)(2,1)} %broadcast_in_dim.19), calls=%async_computation | async-start | bytes 2097152 | tf_op jit(solution)/shard_map/all_to_all | solution.py:15
  130.5 1.0 copy-start.3
  130.6 1.4 copy-start.5
  132.4 1.4 copy-start.7
  134.2 1.2 copy-start.1
  135.4 1.0 copy-start
Sparse Core Ops, SparseCore 0:
  9.4 75.7 all-gather.10
  87.4 68.2 all-gather.8
  157.8 67.7 all-gather.6
where the time goes:
time: 239 us; the launch traced here: 238 us
  waiting for transfers between devices  116 us (49%)
  starting transfers between devices  41.5 us (17%)
  other arithmetic  39.4 us (16%)
  local copies, waits for them, and re-layouts  14.8 us (6%)
  between operations  13.7 us (6%)
  matrix products  12.3 us (5%)
    all_gather x3, waiting for transfers between devices, per_device(): lax.all_gather(local_volts, 'row', axis=1, tiled=True)  83.1 us
    all_to_all x6, starting transfers between devices, sent_to_all(): return lax.all_to_all(copies, axis, split_axis=0, concat_axis=0, tiled=True)  41.4 us
    all_to_all x6, waiting for transfers between devices, sent_to_all(): return lax.all_to_all(copies, axis, split_axis=0, concat_axis=0, tiled=True)  31.4 us
    another operation x9, other arithmetic, subtract(): lower_factor = jnp.linalg.cholesky(system)  19.7 us
    another operation x6, other arithmetic, subtract(): lax.linalg.triangular_solve(lower_factor, middle, left_side=True, lower=T...  16.6 us
    dot_general x9, matrix products, correlate(): jnp.einsum('xn,yn->xy', stacked_first, stacked_second, preferred_element_...  7.67 us
    broadcast_in_dim x6, local copies, waits for them, and re-layouts, sent_to_all(): copies = jnp.broadcast_to(x, (lax.axis_size(axis), *x.shape))  5.59 us
  transfers between devices with their start and end apart: 9, of which 6 were waited for; matrix products, arithmetic and copies ran while one was open for 24% of the time, Pallas kernels for 0%

commit v1 on v0

--- a/solution.py
+++ b/solution.py
@@ -68,7 +68,10 @@
         width_rows = row_volts.shape[1]
         left_factor_matrix = jnp.concatenate([row_volts, ref_all], 1)
         joined = correlate(
-            left_factor_matrix, lax.all_gather(local_volts, "row", axis=1, tiled=True)
+            left_factor_matrix,
+            jnp.concatenate(
+                lax.all_to_all(jnp.stack([local_volts] * lax.axis_size("row")), "row", 0, 0), axis=1
+            ),
         )
         vis_tile = joined[:, :width_rows]
         cross_cols = joined[:, width_rows:]

time: 239 us -> 301 us (1.26)
  the two profiles are of different devices: /device:TPU:2 before, /device:TPU:32 now
where the time goes in v1:
time: 301 us; the launch traced here: 300 us
  waiting for transfers between devices  112 us (37%)
  blocking collectives  72 us (24%)
  other arithmetic  47.3 us (16%)
  starting transfers between devices  40.1 us (13%)
  local copies, waits for them, and re-layouts  19 us (6%)
  matrix products  8.22 us (3%)
    all_to_all x3, waiting for transfers between devices, per_device(): lax.all_to_all(jnp.stack([local_volts] * lax.axis_size('row')), 'row', 0, 0)  86 us
    all_to_all x4, blocking collectives, sent_to_all(): return lax.all_to_all(copies, axis, split_axis=0, concat_axis=0, tiled=True)  72 us
    all_to_all x3, starting transfers between devices, per_device(): lax.all_to_all(jnp.stack([local_volts] * lax.axis_size('row')), 'row', 0, 0)  32.3 us
    all_to_all x2, waiting for transfers between devices, sent_to_all(): return lax.all_to_all(copies, axis, split_axis=0, concat_axis=0, tiled=True)  26.4 us
    another operation x6, other arithmetic, subtract(): lax.linalg.triangular_solve(lower_factor, middle, left_side=True, lower=T...  20.5 us
    another operation x9, other arithmetic, subtract(): lower_factor = jnp.linalg.cholesky(system)  20.4 us
    all_to_all x2, starting transfers between devices, sent_to_all(): return lax.all_to_all(copies, axis, split_axis=0, concat_axis=0, tiled=True)  7.85 us
  transfers between devices with their start and end apart: 5, of which 5 were waited for; matrix products, arithmetic and copies ran while one was open for 20% of the time, Pallas kernels for 0%

profile of v1, /device:TPU:32, one launch (start us, length us, event | category | flops | bytes accessed | tf_op | source)
XLA Modules:
  0.0 299.7 jit_solution(1724184283934996901)
XLA Ops:
  0.0 0.8 slice_bitcast_fusion.23
  0.8 16.2 %all_to_all.45 = bf16[16,2,32,128]{3,2,1,0:T(8,128)(2,1)S(1)} all-to-all(bf16[16,2,32,128]{3,2,1,0:T(8,128)(2,1)S(1)} %broadcast_in_dim.20), channel_id=1, replica_groups=mesh['row'=16,'col'=16,'chan'=2] {'col'}, dimensions={0} | all-to-all | bytes 524288 | tf_op jit(solution)/shard_map/all_to_all | solution.py:15
  17.1 12.7 %all_to_all.46 = bf16[16,2,32,128]{3,2,1,0:T(8,128)(2,1)} all-to-all(bf16[16,2,32,128]{3,2,1,0:T(8,128)(2,1)S(1)} %broadcast_in_dim.24), channel_id=1, replica_groups=mesh['row'=16,'col'=16,'chan'=2] {'col'}, dimensions={0} | all-to-all | bytes 524288 | tf_op jit(solution)/shard_map/all_to_all | solution.py:15
  29.8 0.8 broadcast_in_dim.22
  30.5 4.2 %all-to-all-start.4 = ((bf16[16,2,32,128]{3,2,1,0:T(8,128)(2,1)}), bf16[16,2,32,128]{3,2,1,0:T(8,128)(2,1)}, u32[]{:S(2)}, u32[]{:S(2)}) async-start(bf16[16,2,32,128]{3,2,1,0:T(8,128)(2,1)} %broadcast_in_dim.22), calls=%async_computation.4 | async-start | bytes 524288 | tf_op jit(solution)/shard_map/all_to_all | solution.py:15
  34.8 9.4 %all-to-all-done.4 = bf16[16,2,32,128]{3,2,1,0:T(8,128)(2,1)} async-done(((bf16[16,2,32,128]{3,2,1,0:T(8,128)(2,1)}), bf16[16,2,32,128]{3,2,1,0:T(8,128)(2,1)}, u32[]{:S(2)}, u32[]{:S(2)}) %all-to-all-start.4) | async-done | bytes 262176 | tf_op jit(solution)/shard_map/all_to_all | solution.py:15
  44.1 1.1 broadcast_in_dim.19
  45.2 21.6 %all_to_all.47 = bf16[16,2,8,2048]{3,2,1,0:T(8,128)(2,1)S(1)} all-to-all(bf16[16,2,8,2048]{3,2,1,0:T(8,128)(2,1)} %broadcast_in_dim.19), channel_id=1, replica_groups=mesh['row'=16,'col'=16,'chan'=2] {'col'}, dimensions={0} | all-to-all | bytes 2097152 | tf_op jit(solution)/shard_map/all_to_all | solution.py:15
  66.8 1.1 broadcast_in_dim.23
  67.9 21.6 %all_to_all.48 = bf16[16,2,8,2048]{3,2,1,0:T(8,128)(2,1)S(1)} all-to-all(bf16[16,2,8,2048]{3,2,1,0:T(8,128)(2,1)} %broadcast_in_dim.23), channel_id=1, replica_groups=mesh['row'=16,'col'=16,'chan'=2] {'col'}, dimensions={0} | all-to-all | bytes 2097152 | tf_op jit(solution)/shard_map/all_to_all | solution.py:15
  89.5 1.1 broadcast_in_dim.21
  90.6 3.7 %all-to-all-start.3 = ((bf16[16,2,8,2048]{3,2,1,0:T(8,128)(2,1)}), bf16[16,2,8,2048]{3,2,1,0:T(8,128)(2,1)S(1)}, u32[]{:S(2)}, u32[]{:S(2)}) async-start(bf16[16,2,8,2048]{3,2,1,0:T(8,128)(2,1)} %broadcast_in_dim.21), calls=%async_computation.3 | async-start | bytes 2097152 | tf_op jit(solution)/shard_map/all_to_all | solution.py:15
  94.7 0.4 copy-done.6
  95.1 17.1 %all-to-all-done.3 = bf16[16,2,8,2048]{3,2,1,0:T(8,128)(2,1)S(1)} async-done(((bf16[16,2,8,2048]{3,2,1,0:T(8,128)(2,1)}), bf16[16,2,8,2048]{3,2,1,0:T(8,128)(2,1)S(1)}, u32[]{:S(2)}, u32[]{:S(2)}) %all-to-all-start.3) | async-done | bytes 1048608 | tf_op jit(solution)/shard_map/all_to_all | solution.py:15
  112.2 1.0 copy-done.2
  113.2 15.2 %all-to-all-start.2 = ((bf16[16,2,8,2048]{3,2,1,0:T(8,128)(2,1)}), bf16[16,2,8,2048]{3,2,1,0:T(8,128)(2,1)S(1)}, u32[]{:S(2)}, u32[]{:S(2)}) async-start(bf16[16,2,8,2048]{3,2,1,0:T(8,128)(2,1)} %broadcast_in_dim.19), calls=%async_computation.2 | async-start | bytes 2097152 | tf_op jit(solution)/shard_map/all_to_all | solution.py:73
  128.6 5.9 %cholesky.59 = f32[64,64]{1,0:T(8,128)S(1)} custom-call(f32[64,64]{1,0:T(8,128)S(1)} %fusion.59), custom_call_target="Cholesky" | custom-call | tf_op jit(solution)/shard_map/jit(cholesky)/cholesky | solution.py:42
  134.5 1.1 copy.76
  136.1 0.7 fusion.51
  136.8 6.6 %cholesky.81 = f32[64,64]{1,0:T(8,128)S(1)} custom-call(f32[64,64]{1,0:T(8,128)} %fusion.51), custom_call_target="Cholesky" | custom-call | tf_op jit(solution)/shard_map/jit(cholesky)/cholesky | solution.py:42
  143.4 1.1 copy.67
  144.9 0.4 copy-done.10
  145.3 0.7 maximum_maximum_fusion.1
  146.0 0.9 copy.74
  146.9 0.7 compare_reduce_fusion.2
  147.6 0.7 compare_reduce_fusion
  148.3 1.2 fusion.33
  149.5 1.2 fusion.35
  150.7 26.8 %all-to-all-done.2 = bf16[16,2,8,2048]{3,2,1,0:T(8,128)(2,1)S(1)} async-done(((bf16[16,2,8,2048]{3,2,1,0:T(8,128)(2,1)}), bf16[16,2,8,2048]{3,2,1,0:T(8,128)(2,1)S(1)}, u32[]{:S(2)}, u32[]{:S(2)}) %all-to-all-start.2) | async-done | bytes 1048608 | tf_op jit(solution)/shard_map/all_to_all | solution.py:73
  177.5 8.7 %all-to-all-start.8 = ((bf16[16,2,8,2048]{3,2,1,0:T(8,128)(2,1)}), bf16[16,2,8,2048]{3,2,1,0:T(8,128)(2,1)}, u32[]{:S(2)}, u32[]{:S(2)}) async-start(bf16[16,2,8,2048]{3,2,1,0:T(8,128)(2,1)} %broadcast_in_dim.23), calls=%async_computation.8 | async-start | bytes 2097152 | tf_op jit(solution)/shard_map/all_to_all | solution.py:73
  186.3 6.3 %custom-call.13 = f32[1,64,64]{1,2,0:T(8,128)} custom-call(f32[1,64,64]{2,1,0:T(8,128)} %fusion.33), custom_call_target="InvertDiagBlocksLowerTriangular" | custom-call | tf_op jit(solution)/shard_map/triangular_solve/custom-call.2 | solution.py:45
  192.6 6.3 %custom-call.17 = f32[1,64,64]{1,2,0:T(8,128)} custom-call(f32[1,64,64]{2,1,0:T(8,128)} %fusion.35), custom_call_target="InvertDiagBlocksLowerTriangular" | custom-call | tf_op jit(solution)/shard_map/triangular_solve/custom-call.2 | solution.py:45
  198.8 5.8 %cholesky.70 = f32[64,64]{1,0:T(8,128)S(1)} custom-call(f32[64,64]{1,0:T(8,128)S(1)} %fusion.55), custom_call_target="Cholesky" | custom-call | tf_op jit(solution)/shard_map/jit(cholesky)/cholesky | solution.py:42
  204.7 0.7 compare_reduce_fusion.1
  205.4 0.6 fusion.34
  206.0 4.9 %custom-call.15 = f32[1,64,64]{1,2,0:T(8,128)S(1)} custom-call(f32[1,64,64]{2,1,0:T(8,128)S(1)} %fusion.34), custom_call_target="InvertDiagBlocksLowerTriangular" | custom-call | tf_op jit(solution)/shard_map/triangular_solve/custom-call.2 | solution.py:45
  211.0 1.0 copy_bitcast_fusion
  212.0 1.7 copy_bitcast_fusion.1
  213.8 1.1 copy-done.3
  215.1 0.8 copy-done.7
  215.9 0.4 fusion.16
  216.4 0.4 fusion.8
  216.9 0.4 fusion.12
  217.3 1.1 pad_maximum_fusion
  218.5 1.2 pad_maximum_fusion.2
  219.6 16.4 %all-to-all-done.8 = bf16[16,2,8,2048]{3,2,1,0:T(8,128)(2,1)} async-done(((bf16[16,2,8,2048]{3,2,1,0:T(8,128)(2,1)}), bf16[16,2,8,2048]{3,2,1,0:T(8,128)(2,1)}, u32[]{:S(2)}, u32[]{:S(2)}) %all-to-all-start.8) | async-done | bytes 1048608 | tf_op jit(solution)/shard_map/all_to_all | solution.py:73
  236.0 8.4 %all-to-all-start.5 = ((bf16[16,2,8,2048]{3,2,1,0:T(8,128)(2,1)}), bf16[16,2,8,2048]{3,2,1,0:T(8,128)(2,1)}, u32[]{:S(2)}, u32[]{:S(2)}) async-start(bf16[16,2,8,2048]{3,2,1,0:T(8,128)(2,1)} %broadcast_in_dim.21), calls=%async_computation.5 | async-start | bytes 2097152 | tf_op jit(solution)/shard_map/all_to_all | solution.py:73
  244.4 1.1 pad_maximum_fusion.1
  245.6 1.4 copy.77
  247.2 0.5 fusion.99
  247.8 0.7 copy-done
  248.5 0.5 fusion.101
  251.3 42.8 %all-to-all-done.5 = bf16[16,2,8,2048]{3,2,1,0:T(8,128)(2,1)} async-done(((bf16[16,2,8,2048]{3,2,1,0:T(8,128)(2,1)}), bf16[16,2,8,2048]{3,2,1,0:T(8,128)(2,1)}, u32[]{:S(2)}, u32[]{:S(2)}) %all-to-all-start.5) | async-done | bytes 1048608 | tf_op jit(solution)/shard_map/all_to_all | solution.py:73
  294.1 1.3 copy.68
  295.4 0.5 fusion.100
  296.4 0.3 fusion.74
  296.7 0.3 fusion.75
  297.0 0.3 fusion.4
  297.3 0.3 fusion.5
  297.6 0.3 fusion
  297.9 0.3 fusion.1
  298.2 0.3 fusion.2
  298.5 0.3 fusion.3
  298.9 0.8 pad_maximum_fusion.3
  (84 shorter events, 5.1 us)
Async XLA Ops:
  0.0 34.7 %copy-start.12 = (bf16[3,2,8,2048]{3,2,1,0:T(8,128)(2,1)S(1)}, bf16[3,2,8,2048]{3,2,1,0:T(8,128)(2,1)}, u32[]{:S(2)}) copy-start(bf16[3,2,8,2048]{3,2,1,0:T(8,128)(2,1)} %param.7) | copy-start | bytes 589828
  17.1 77.2 %copy-start.4 = (bf16[16,2,32,128]{3,2,1,0:T(8,128)(2,1)}, bf16[16,2,32,128]{3,2,1,0:T(8,128)(2,1)S(1)}, u32[]{:S(2)}) copy-start(bf16[16,2,32,128]{3,2,1,0:T(8,128)(2,1)S(1)} %all_to_all.45) | copy-start | bytes 786436
  30.5 13.6 %all-to-all-start.4 = ((bf16[16,2,32,128]{3,2,1,0:T(8,128)(2,1)}), bf16[16,2,32,128]{3,2,1,0:T(8,128)(2,1)}, u32[]{:S(2)}, u32[]{:S(2)}) async-start(bf16[16,2,32,128]{3,2,1,0:T(8,128)(2,1)} %broadcast_in_dim.22), calls=%async_computation.4 | async-start | bytes 524288 | tf_op jit(solution)/shard_map/all_to_all | solution.py:15
  90.6 21.6 %all-to-all-start.3 = ((bf16[16,2,8,2048]{3,2,1,0:T(8,128)(2,1)}), bf16[16,2,8,2048]{3,2,1,0:T(8,128)(2,1)S(1)}, u32[]{:S(2)}, u32[]{:S(2)}) async-start(bf16[16,2,8,2048]{3,2,1,0:T(8,128)(2,1)} %broadcast_in_dim.21), calls=%async_computation.3 | async-start | bytes 2097152 | tf_op jit(solution)/shard_map/all_to_all | solution.py:15
  94.4 0.7 copy-start.6
  112.2 1.0 copy-start.2
  113.2 64.4 %all-to-all-start.2 = ((bf16[16,2,8,2048]{3,2,1,0:T(8,128)(2,1)}), bf16[16,2,8,2048]{3,2,1,0:T(8,128)(2,1)S(1)}, u32[]{:S(2)}, u32[]{:S(2)}) async-start(bf16[16,2,8,2048]{3,2,1,0:T(8,128)(2,1)} %broadcast_in_dim.19), calls=%async_computation.2 | async-start | bytes 2097152 | tf_op jit(solution)/shard_map/all_to_all | solution.py:73
  135.6 9.3 %copy-start.8 = (bf16[2,32,16,128]{3,2,1,0:T(8,128)(2,1)}, bf16[2,32,16,128]{3,2,1,0:T(8,128)(2,1)S(1)}, u32[]{:S(2)}) copy-start(bf16[2,32,16,128]{3,2,1,0:T(8,128)(2,1)S(1)} %copy.76) | copy-start | bytes 786436
  144.6 0.7 copy-start.10
  146.0 65.0 %copy-start.5 = (bf16[16,2,32,128]{3,2,1,0:T(8,128)(2,1)S(1)}, bf16[16,2,32,128]{3,2,1,0:T(8,128)(2,1)}, u32[]{:S(2)}) copy-start(bf16[16,2,32,128]{3,2,1,0:T(8,128)(2,1)} %copy-done.4) | copy-start | bytes 786436
  177.5 58.4 %all-to-all-start.8 = ((bf16[16,2,8,2048]{3,2,1,0:T(8,128)(2,1)}), bf16[16,2,8,2048]{3,2,1,0:T(8,128)(2,1)}, u32[]{:S(2)}, u32[]{:S(2)}) async-start(bf16[16,2,8,2048]{3,2,1,0:T(8,128)(2,1)} %broadcast_in_dim.23), calls=%async_computation.8 | async-start | bytes 2097152 | tf_op jit(solution)/shard_map/all_to_all | solution.py:73
  213.7 1.2 copy-start.3
  214.9 0.9 copy-start.7
  215.0 1.4 copy-start.9
  215.9 1.0 copy-start.11
  236.0 58.2 %all-to-all-start.5 = ((bf16[16,2,8,2048]{3,2,1,0:T(8,128)(2,1)}), bf16[16,2,8,2048]{3,2,1,0:T(8,128)(2,1)}, u32[]{:S(2)}, u32[]{:S(2)}) async-start(bf16[16,2,8,2048]{3,2,1,0:T(8,128)(2,1)} %broadcast_in_dim.21), calls=%async_computation.5 | async-start | bytes 2097152 | tf_op jit(solution)/shard_map/all_to_all | solution.py:73
  245.6 1.6 copy-start.1
  247.2 1.3 copy-start
  248.5 0.8 copy-start.14
  248.5 1.0 copy-start.13
